TPU v7x, 32 devices: a whole 2x2x4 slice. The times are simulated.
32 devices in a mesh: chain: 4 (over z), param: 8 (over y, x, core).
Axes of the slice: x: 2, y: 2, z: 4, core: 2. Of those that a mesh axis runs over, the one named last changes fastest.
Arguments:
- spins: int32 [128, 256, 4], P(('chain', 'param')), may hold values from 0 to 1
- local_energy: float32 [128], replicated, may hold values from -24 to 24
- embed_weight: float32 [4, 256], replicated, may hold values from -3 to 3
- position: bfloat16 [256, 256], replicated, may hold values from -6 to 6
- value_weight: bfloat16 [256, 256], replicated, may hold values from -0.375 to 0.375
- mixing: bfloat16 [8, 256, 256], replicated, may hold values from -0.375 to 0.375
- out_weight: bfloat16 [256, 256], replicated, may hold values from -0.375 to 0.375
- up_weight: bfloat16 [256, 1024], replicated, may hold values from -0.375 to 0.375
- down_weight: bfloat16 [1024, 256], replicated, may hold values from -0.1875 to 0.1875
- readout: float32 [256], replicated, may hold values from -6 to 6
Outputs:
- up_update: float32 [256, 1024], P('chain', 'param')
- down_update: float32 [1024, 256], P('param', 'chain')
- sample_weights: float32 [128], replicated
All inputs are finite; a program needn't handle non-finite values.
Results may differ from a plain program's by a relative error of at most 0.018.
Values may be sent and summed in bfloat16 or wider, within the bound.
A program may use at most 128 MiB of HBM per device.

v0:
```python
import math
import jax
import jax.numpy as jnp
from jax import lax
from jax.sharding import PartitionSpec as P

damping = 0.05


def layer_norm(hidden_state):
    average = jnp.mean(hidden_state, axis=-1, keepdims=True)
    centred = hidden_state - average
    spread = jnp.mean(centred * centred, axis=-1, keepdims=True)
    return centred * lax.rsqrt(spread + 1e-05)


def project(operand, weights):
    return lax.dot_general(
        operand,
        weights,
        (((operand.ndim - 1,), (0,)), ((), ())),
        preferred_element_type=jnp.float32,
    )


def center_rows(jacobian, total):
    jac_wide = jacobian.astype(jnp.float32)
    return (jac_wide - jnp.mean(jac_wide, axis=0)) / math.sqrt(total)


def gram_of(centred, total):
    flat = centred.reshape(total, -1)
    return lax.dot_general(
        flat,
        flat,
        (((1,), (1,)), ((), ())),
        precision=lax.Precision.HIGHEST,
        preferred_element_type=jnp.float32,
    )


def solve_weights(gram, local_energy, total):
    scale = jnp.trace(gram) / total
    system = gram + damping * scale * jnp.eye(total, dtype=jnp.float32)
    lower = jnp.linalg.cholesky(system)
    energy = (local_energy - jnp.mean(local_energy)) / math.sqrt(total)
    column = energy[:, None]
    middle = lax.linalg.triangular_solve(lower, column, left_side=True, lower=True)
    answer = lax.linalg.triangular_solve(
        lower, middle, left_side=True, lower=True, transpose_a=True
    )
    return scale * answer[:, 0]


def body(
    spins,
    local_energy,
    embed_weight,
    position,
    value_weight,
    mixing,
    out_weight,
    up_weight,
    down_weight,
    readout,
):
    samples = spins.shape[0]
    patch_rows = spins.shape[1]
    total = local_energy.shape[0]
    head_count = mixing.shape[0]
    model_width = value_weight.shape[0]
    spin_values = (2 * spins - 1).astype(jnp.float32)
    embedded = jnp.sum(spin_values[..., None] * embed_weight, axis=2) + position.astype(jnp.float32)
    normed = layer_norm(embedded).astype(jnp.bfloat16)
    values = project(normed, value_weight).astype(jnp.bfloat16)
    split_values = values.reshape(samples, patch_rows, head_count, model_width // head_count)
    mixture = jnp.einsum("htu,suhe->sthe", mixing, split_values, preferred_element_type=jnp.float32)
    mixture = mixture.astype(jnp.bfloat16).reshape(samples, patch_rows, model_width)
    residual = embedded + project(mixture, out_weight)
    features = layer_norm(residual).astype(jnp.bfloat16)
    preact = project(features, up_weight)
    hidden = jax.nn.gelu(preact).astype(jnp.bfloat16)
    output = residual + project(hidden, down_weight)
    cotangent = (readout * jnp.tanh(output)).astype(jnp.bfloat16)
    backward = lax.dot_general(
        cotangent, down_weight, (((2,), (1,)), ((), ())), preferred_element_type=jnp.float32
    )
    preact_grad = jax.vjp(jax.nn.gelu, preact)[1](backward)[0].astype(jnp.bfloat16)
    up_block = jnp.einsum("sti,stj->sij", features, preact_grad, preferred_element_type=jnp.float32)
    down_block = jnp.einsum("std,stj->sdj", cotangent, hidden, preferred_element_type=jnp.float32)
    jacobian = jnp.stack([up_block, down_block], axis=1).astype(jnp.bfloat16)
    grouped = lax.all_to_all(jacobian, "param", split_axis=3, concat_axis=0, tiled=True)
    chosen_raw = lax.all_to_all(grouped, "chain", split_axis=2, concat_axis=0, tiled=True)
    centred = center_rows(chosen_raw, total)
    gram = lax.psum(gram_of(centred, total), ("chain", "param"))
    sample_weights = solve_weights(gram, local_energy, total)
    update = -lax.dot_general(
        sample_weights,
        centred,
        (((0,), (0,)), ((), ())),
        precision=lax.Precision.HIGHEST,
        preferred_element_type=jnp.float32,
    )
    return (update[0], update[1].T, sample_weights)


def solution(mesh):
    in_specs = (P(("chain", "param"), None, None), P(), P(), P(), P(), P(), P(), P(), P(), P())
    out_specs = (P("chain", "param"), P("param", "chain"), P())
    return jax.shard_map(body, mesh=mesh, in_specs=in_specs, out_specs=out_specs, check_vma=False)
```

profile of v0, /device:TPU:1, one launch (start us, length us, event | category | flops | bytes accessed | tf_op | source)
XLA Modules:
  0.0 412.8 jit_solution(4878717197872433788)
XLA Ops:
  8.1 1.5 multiply_reduce_fusion
  9.9 1.0 copy.90
  13.5 1.9 copy-done.3
  15.4 2.5 fusion.16
  17.9 6.1 %convert_bitcast_fusion.2 = bf16[4,1,256,1024]{3,2,0,1:T(8,128)(2,1)S(1)} fusion(f32[4,256,1024]{2,1,0:T(8,128)} %copy-done.3, bf16[4,256,256]{1,2,0:T(8,128)(2,1)} %fusion.16, bf16[1024,256]{1,0:T(8,128)(2,1)} %param.18, f32[4,256,256]{1,2,0:T(8,128)S(1)} %get-tuple-element.6, f32[4,256]{1,0:T(4,128)S(1)} %add_rsqrt_fusion, ...), kind=kOutput, calls=%fused_computation.21 | convolution fusion | flops 1096548352 | bytes 8396800 | tf_op jit(solution)/shard_map/sti,stj->sij/dot_general | solution.py:89
  24.0 4.1 convert_bitcast_fusion.1
  28.1 2.3 pad_maximum_fusion
  30.4 7.8 %copy.101 = bf16[4,2,256,1024]{2,0,1,3:T(4,128)(2,1)} copy(bf16[4,2,256,1024]{3,2,0,1:T(8,128)(2,1)} %pad_maximum_fusion) | data formatting | bytes 8388608 | tf_op jit(solution)/shard_map/stack | solution.py:91
  38.2 53.2 %all_to_all.27 = bf16[4,2,256,1024]{2,0,1,3:T(4,128)(2,1)S(1)} all-to-all(bf16[4,2,256,1024]{2,0,1,3:T(4,128)(2,1)} %copy.101), channel_id=1, replica_groups=mesh['chain'=4,'param'=8] {'param'}, dimensions={3} | all-to-all | bytes 8388608 | tf_op jit(solution)/shard_map/all_to_all | solution.py:92
  91.4 2.8 copy.102
  94.2 6.5 %copy.103 = bf16[8,4,2,256,128]{4,3,2,1,0:T(8,128)(2,1)} copy(bf16[8,4,2,256,128]{3,4,0,2,1:T(8,128)(2,1)} %bitcast.90) | data formatting | bytes 8388608 | tf_op jit(solution)/shard_map/all_to_all | solution.py:92
  100.6 6.5 %copy.104 = bf16[32,2,256,128]{3,1,0,2:T(2,128)(2,1)S(1)} copy(bf16[32,2,256,128]{3,2,1,0:T(8,128)(2,1)} %bitcast.91) | data formatting | bytes 8388608 | tf_op jit(solution)/shard_map/all_to_all | solution.py:92
  107.2 96.8 %all_to_all.28 = bf16[32,2,256,128]{3,1,0,2:T(2,128)(2,1)S(1)} all-to-all(bf16[32,2,256,128]{3,1,0,2:T(2,128)(2,1)S(1)} %copy.104), channel_id=1, replica_groups=mesh['chain'=4,'param'=8] {'chain'}, dimensions={2} | all-to-all | bytes 8388608 | tf_op jit(solution)/shard_map/all_to_all | solution.py:93
  203.9 4.9 %copy.105 = bf16[32,2,256,128]{3,2,1,0:T(8,128)(2,1)S(1)} copy(bf16[32,2,256,128]{3,1,0,2:T(2,128)(2,1)S(1)} %all_to_all.28) | data formatting | bytes 8388608 | tf_op jit(solution)/shard_map/all_to_all | solution.py:93
  209.6 5.4 %fusion.2 = f32[4,32,2,64,128]{4,3,0,2,1:T(8,128)S(1)} fusion(f32[2,64,128]{2,1,0:T(8,128)S(1)} %broadcast_multiply_fusion, bf16[32,2,256,128]{3,1,0,2:T(2,128)(2,1)S(1)} %all_to_all.28), kind=kLoop, calls=%fused_computation.3 | loop fusion | flops 6291456 | bytes 12648448 | tf_op jit(solution)/shard_map/div | solution.py:28
  215.0 10.4 %copy.106 = f32[4,32,2,64,128]{4,3,2,1,0:T(8,128)S(1)} copy(f32[4,32,2,64,128]{4,3,0,2,1:T(8,128)S(1)} %fusion.2) | data formatting | bytes 16777216 | tf_op jit(solution)/shard_map/div | solution.py:28
  225.4 3.2 copy-done.2
  228.7 17.1 %fusion.18 = f32[128,128]{1,0:T(8,128)} fusion(f32[128,2,64,128]{3,2,1,0:T(8,128)S(1)} %bitcast.88), kind=kOutput, calls=%fused_computation.30 | convolution fusion | flops 3221225472 | bytes 8454144 | tf_op jit(solution)/shard_map/dot_general | solution.py:33
  247.1 117.5 %all-reduce.2.cloned.1.call-done = f32[128,128]{1,0:T(8,128)} async-done(((f32[128,128]{1,0:T(8,128)}), f32[128,128]{1,0:T(8,128)}) %all-reduce.2.cloned.1.call-update) | async-done | bytes 65552 | tf_op jit(solution)/shard_map/psum | solution.py:95
  364.5 1.5 select_reduce_fusion.1
  368.2 0.9 fusion.37
  369.1 11.7 %cholesky.13 = f32[128,128]{1,0:T(8,128)S(1)} custom-call(f32[128,128]{1,0:T(8,128)S(1)} %fusion.37), custom_call_target="Cholesky" | custom-call | tf_op jit(solution)/shard_map/jit(cholesky)/cholesky | solution.py:45
  382.1 9.8 %custom-call.8 = f32[1,128,128]{1,2,0:T(8,128)S(1)} custom-call(f32[1,128,128]{2,1,0:T(8,128)S(1)} %fusion.34), custom_call_target="InvertDiagBlocksLowerTriangular" | custom-call | tf_op jit(solution)/shard_map/triangular_solve | solution.py:49
  392.3 12.5 %fusion.3 = f32[1,2,64,128]{3,0,2,1:T(1,128)S(1)} fusion(f32[128,2,64,128]{3,2,1,0:T(8,128)} %bitcast.89, f32[128]{0:T(128)S(1)} %fusion.21), kind=kOutput, calls=%fused_computation.4 | convolution fusion | flops 25165824 | bytes 8454656 | tf_op jit(solution)/shard_map/dot_general | solution.py:97
  (48 shorter events, 8.3 us)
Async XLA Ops:
  7.2 4.4 %copy-start = (bf16[8,256,256]{2,1,0:T(8,128)(2,1)S(1)}, bf16[8,256,256]{2,1,0:T(8,128)(2,1)}, u32[]{:S(2)}) copy-start(bf16[8,256,256]{2,1,0:T(8,128)(2,1)} %param.15) | copy-start | bytes 3145732
  7.2 4.0 copy-start.6
  7.2 357.3 %all-reduce.2.cloned.1.call-start = ((), (), s32[]{:S(2)}) async-start(), calls=%async_computation.2 | async-start | bytes 131072 | tf_op jit(solution)/shard_map/psum | solution.py:95
  9.9 2.3 copy-start.5
  11.2 1.5 copy-start.4
  12.1 3.2 copy-start.9
  12.2 3.2 copy-start.10
  13.4 1.9 copy-start.3
  225.4 3.2 copy-start.2
  228.7 17.1 %copy-start.8 = (f32[128]{0:T(128)S(1)}, f32[128]{0:T(128)}, u32[]{:S(2)}) copy-start(f32[128]{0:T(128)} %param.11) | copy-start | bytes 1540
  392.1 13.4 %copy-start.1 = (bf16[8,256,256]{2,1,0:T(8,128)(2,1)S(1)}, bf16[8,256,256]{2,1,0:T(8,128)(2,1)}, u32[]{:S(2)}) copy-start(bf16[8,256,256]{2,1,0:T(8,128)(2,1)} %param.15) | copy-start | bytes 3145732
  392.3 12.5 %copy-start.7 = (f32[128]{0:T(128)}, f32[128]{0:T(128)S(1)}, u32[]{:S(2)}) copy-start(f32[128]{0:T(128)S(1)} %fusion.21) | copy-start | bytes 1540
Sparse Core Ops, SparseCore 0:
  245.9 118.5 all-reduce.1
where the time goes:
time: 421 us; the launch traced here: 413 us
  blocking collectives  150 us (36%)
  waiting for transfers between devices  117 us (28%)
  local copies, waits for them, and re-layouts  46.1 us (11%)
  matrix products  44.6 us (11%)
  other arithmetic  37.8 us (9%)
  between operations  16.7 us (4%)
    psum x1, waiting for transfers between devices, body(): gram = lax.psum(gram_of(centred, total), ('chain', 'param'))  117 us
    all_to_all x1, blocking collectives, body(): lax.all_to_all(grouped, 'chain', split_axis=2, concat_axis=0, tiled=True)  96.8 us
    all_to_all x1, blocking collectives, body(): lax.all_to_all(jacobian, 'param', split_axis=3, concat_axis=0, tiled=True)  53.2 us
    dot_general x1, matrix products, gram_of(): lax.dot_general(flat, flat, (((1,), (1,)), ((), ())), precision=lax.Preci...  17.1 us
    all_to_all x3, local copies, waits for them, and re-layouts, body(): lax.all_to_all(jacobian, 'param', split_axis=3, concat_axis=0, tiled=True)  15.7 us
    dot_general x1, matrix products, body(): lax.dot_general(sample_weights, centred, (((0,), (0,)), ((), ())), precis...  12.5 us
    another operation x3, other arithmetic, solve_weights(): lower = jnp.linalg.cholesky(system)  12.4 us
    another operation x2, other arithmetic, solve_weights(): lax.linalg.triangular_solve(lower, middle, left_side=True, lower=True, tr...  10.5 us
  transfers between devices with their start and end apart: 1, of which 1 were waited for; matrix products, arithmetic and copies ran while one was open for 0% of the time, Pallas kernels for 0%

commit v1 on v0

--- a/solution.py
+++ b/solution.py
@@ -89,7 +89,19 @@
     up_block = jnp.einsum("sti,stj->sij", features, preact_grad, preferred_element_type=jnp.float32)
     down_block = jnp.einsum("std,stj->sdj", cotangent, hidden, preferred_element_type=jnp.float32)
     jacobian = jnp.stack([up_block, down_block], axis=1).astype(jnp.bfloat16)
-    grouped = lax.all_to_all(jacobian, "param", split_axis=3, concat_axis=0, tiled=True)
+    ways, here = (lax.axis_size("param"), lax.axis_index("param"))
+    width = jacobian.shape[3] // ways
+    shape = list(jacobian.shape)
+    shape[3] = width
+    height = shape[0]
+    shape[0] = height * ways
+    full = jnp.zeros(shape, jacobian.dtype)
+    for mask in range(ways):
+        part = lax.dynamic_slice_in_dim(jacobian, (here ^ mask) * width, width, axis=3)
+        if mask:
+            part = lax.ppermute(part, "param", [(d, d ^ mask) for d in range(ways)])
+        full = lax.dynamic_update_slice_in_dim(full, part, (here ^ mask) * height, axis=0)
+    grouped = full
     chosen_raw = lax.all_to_all(grouped, "chain", split_axis=2, concat_axis=0, tiled=True)
     centred = center_rows(chosen_raw, total)
     gram = lax.psum(gram_of(centred, total), ("chain", "param"))

time: 421 us -> 389 us (0.924)
  blocking collectives: 150 us -> 97.6 us
  waiting for transfers between devices: 117 us -> 142 us
  local copies, waits for them, and re-layouts: 46.1 us -> 33.8 us
  starting transfers between devices: 0.04 us -> 7.49 us
    all_to_all x1 -> x0, blocking collectives: 53.2 us -> none  [body(): lax.all_to_all(jacobian, 'param', split_axis=3, concat_axis=0, tiled=True)]
    ppermute x0 -> x7, waiting for transfers between devices: none -> 23.5 us  [body(): part = lax.ppermute(part, 'param', [(d, d ^ mask) for d in range(ways)])]
    all_to_all x3 -> x0, local copies, waits for them, and re-layouts: 15.7 us -> none  [body(): lax.all_to_all(jacobian, 'param', split_axis=3, concat_axis=0, tiled=True)]
    dynamic_update_slice x0 -> x8, local copies, waits for them, and re-layouts: none -> 15.3 us  [body(): lax.dynamic_update_slice_in_dim(full, part, (here ^ mask) * height, axis=0)]
    div x1, local copies, waits for them, and re-layouts: 10.4 us -> 1.81 us  [center_rows(): return (jac_wide - jnp.mean(jac_wide, axis=0)) / math.sqrt(total)]
    another operation x1 -> x0, local copies, waits for them, and re-layouts: 7.85 us -> none  [body(): jacobian = jnp.stack([up_block, down_block], axis=1).astype(jnp.bfloat16)]
    ppermute x0 -> x7, starting transfers between devices: none -> 7.45 us  [body(): part = lax.ppermute(part, 'param', [(d, d ^ mask) for d in range(ways)])]
    broadcast_in_dim x0 -> x1, local copies, waits for them, and re-layouts: none -> 6.17 us  [body(): full = jnp.zeros(shape, jacobian.dtype)]
  transfers between devices with their start and end apart: 1 -> 8, of which waited for: 1 -> 3; matrix products, arithmetic and copies ran while one was open for 0% -> 6% of each run, Pallas kernels for 0% -> 0%
where the time goes in v1:
time: 389 us; the launch traced here: 382 us
  waiting for transfers between devices  142 us (37%)
  blocking collectives  97.6 us (25%)
  matrix products  43.4 us (11%)
  other arithmetic  41.6 us (11%)
  local copies, waits for them, and re-layouts  33.8 us (9%)
  between operations  16.8 us (4%)
  starting transfers between devices  7.49 us (2%)
    psum x1, waiting for transfers between devices, body(): gram = lax.psum(gram_of(centred, total), ('chain', 'param'))  118 us
    all_to_all x1, blocking collectives, body(): lax.all_to_all(grouped, 'chain', split_axis=2, concat_axis=0, tiled=True)  97.6 us
    ppermute x7, waiting for transfers between devices, body(): part = lax.ppermute(part, 'param', [(d, d ^ mask) for d in range(ways)])  23.5 us
    dot_general x1, matrix products, gram_of(): lax.dot_general(flat, flat, (((1,), (1,)), ((), ())), precision=lax.Preci...  17.1 us
    dynamic_update_slice x8, local copies, waits for them, and re-layouts, body(): lax.dynamic_update_slice_in_dim(full, part, (here ^ mask) * height, axis=0)  15.3 us
    dot_general x1, matrix products, body(): lax.dot_general(sample_weights, centred, (((0,), (0,)), ((), ())), precis...  12.5 us
    another operation x3, other arithmetic, solve_weights(): lower = jnp.linalg.cholesky(system)  12.4 us
    another operation x2, other arithmetic, solve_weights(): lax.linalg.triangular_solve(lower, middle, left_side=True, lower=True, tr...  10.5 us
  transfers between devices with their start and end apart: 8, of which 3 were waited for; matrix products, arithmetic and copies ran while one was open for 6% of the time, Pallas kernels for 0%

profile of v1, /device:TPU:1, one launch (start us, length us, event | category | flops | bytes accessed | tf_op | source)
XLA Modules:
  0.0 382.2 jit_solution(12246269645339529753)
XLA Ops:
  13.5 1.7 fusion.16
  15.4 3.0 convert_bitcast_fusion.1
  18.5 6.7 %convert_bitcast_fusion.2 = bf16[4,1,256,1024]{3,2,0,1:T(8,128)(2,1)} fusion(f32[4,256,1024]{2,1,0:T(8,128)} %copy-done.3, bf16[4,256,256]{1,2,0:T(8,128)(2,1)S(1)} %fusion.16, bf16[1024,256]{1,0:T(8,128)(2,1)S(1)} %copy-done.13, f32[4,256,256]{1,2,0:T(8,128)S(1)} %get-tuple-element.14, f32[4,256]{1,0:T(4,128)S(1)} %add_rsqrt_fusion, ...), kind=kOutput, calls=%fused_computation.36 | convolution fusion | flops 1096548352 | bytes 8396800 | tf_op jit(solution)/shard_map/sti,stj->sij/dot_general | solution.py:89
  25.3 3.8 fusion.23
  29.1 2.7 collective-permute-start.1
  33.5 2.2 fusion.30
  36.1 6.2 %broadcast_in_dim.6 = bf16[32,2,256,128]{3,1,0,2:T(2,128)(2,1)} broadcast(bf16[]{:T(256)} %constant.88.clone.1), dimensions={} | broadcast | bytes 4194306 | tf_op jit(solution)/shard_map/broadcast_in_dim | solution.py:98
  43.7 2.4 collective-permute-start.5
  46.1 2.4 copy_dynamic-update-slice_fusion.6
  48.8 2.4 copy_dynamic-update-slice_fusion.5
  51.2 4.7 %collective-permute-done.2 = bf16[4,2,256,128]{3,2,0,1:T(8,128)(2,1)} collective-permute-done((bf16[4,2,256,128]{3,2,0,1:T(8,128)(2,1)}, bf16[4,2,256,128]{3,2,0,1:T(8,128)(2,1)}, u32[]{:S(2)}, u32[]{:S(2)}) %collective-permute-start.2) | collective-permute-done | bytes 524320 | tf_op jit(solution)/shard_map/ppermute | solution.py:102
  56.0 2.4 copy_dynamic-update-slice_fusion.4
  58.4 2.4 copy_dynamic-update-slice_fusion.3
  60.9 18.8 %collective-permute-done.4 = bf16[4,2,256,128]{3,2,0,1:T(8,128)(2,1)S(1)} collective-permute-done((bf16[4,2,256,128]{3,2,0,1:T(8,128)(2,1)}, bf16[4,2,256,128]{3,2,0,1:T(8,128)(2,1)S(1)}, u32[]{:S(2)}, u32[]{:S(2)}) %collective-permute-start.4) | collective-permute-done | bytes 524320 | tf_op jit(solution)/shard_map/ppermute | solution.py:102
  83.8 97.6 %all_to_all.4 = bf16[32,2,256,128]{3,1,0,2:T(2,128)(2,1)S(1)} all-to-all(bf16[32,2,256,128]{3,1,0,2:T(2,128)(2,1)} %copy_dynamic-update-slice_fusion), channel_id=1, replica_groups=mesh['chain'=4,'param'=8] {'chain'}, dimensions={2} | all-to-all | bytes 8388608 | tf_op jit(solution)/shard_map/all_to_all | solution.py:105
  181.4 4.9 %copy.109 = bf16[32,2,256,128]{3,2,1,0:T(8,128)(2,1)S(1)} copy(bf16[32,2,256,128]{3,1,0,2:T(2,128)(2,1)S(1)} %all_to_all.4) | data formatting | bytes 8388608 | tf_op jit(solution)/shard_map/all_to_all | solution.py:105
  187.1 5.4 %fusion.2 = f32[4,32,2,64,128]{4,3,0,2,1:T(8,128)S(1)} fusion(f32[2,64,128]{2,1,0:T(8,128)S(1)} %broadcast_multiply_fusion, bf16[32,2,256,128]{3,1,0,2:T(2,128)(2,1)S(1)} %all_to_all.4), kind=kLoop, calls=%fused_computation.3 | loop fusion | flops 6291456 | bytes 12648448 | tf_op jit(solution)/shard_map/div | solution.py:28
  192.5 1.8 copy.110
  194.3 3.2 copy-done.1
  197.5 17.1 %fusion.18 = f32[128,128]{1,0:T(8,128)} fusion(f32[128,2,64,128]{3,2,1,0:T(8,128)S(1)} %bitcast.84), kind=kOutput, calls=%fused_computation.45 | convolution fusion | flops 3221225472 | bytes 8454144 | tf_op jit(solution)/shard_map/dot_general | solution.py:33
  215.9 118.0 %all-reduce.2.cloned.1.call-done = f32[128,128]{1,0:T(8,128)} async-done(((f32[128,128]{1,0:T(8,128)}), f32[128,128]{1,0:T(8,128)}) %all-reduce.2.cloned.1.call-update) | async-done | bytes 65552 | tf_op jit(solution)/shard_map/psum | solution.py:107
  338.5 11.7 %cholesky.13 = f32[128,128]{1,0:T(8,128)S(1)} custom-call(f32[128,128]{1,0:T(8,128)S(1)} %fusion.45), custom_call_target="Cholesky" | custom-call | tf_op jit(solution)/shard_map/jit(cholesky)/cholesky | solution.py:45
  351.6 9.8 %custom-call.8 = f32[1,128,128]{1,2,0:T(8,128)S(1)} custom-call(f32[1,128,128]{2,1,0:T(8,128)S(1)} %fusion.42), custom_call_target="InvertDiagBlocksLowerTriangular" | custom-call | tf_op jit(solution)/shard_map/triangular_solve | solution.py:49
  361.7 12.5 %fusion.3 = f32[1,2,64,128]{3,0,2,1:T(1,128)S(1)} fusion(f32[128,2,64,128]{3,2,1,0:T(8,128)} %bitcast.85, f32[128]{0:T(128)S(1)} %fusion.21), kind=kOutput, calls=%fused_computation.20 | convolution fusion | flops 25165824 | bytes 8454656 | tf_op jit(solution)/shard_map/dot_general | solution.py:109
  (75 shorter events, 21.4 us)
Async XLA Ops:
  7.2 4.4 %copy-start = (bf16[8,256,256]{2,1,0:T(8,128)(2,1)S(1)}, bf16[8,256,256]{2,1,0:T(8,128)(2,1)}, u32[]{:S(2)}) copy-start(bf16[8,256,256]{2,1,0:T(8,128)(2,1)} %param.15) | copy-start | bytes 3145732
  7.2 4.0 %copy-start.9 = (bf16[256,256]{1,0:T(8,128)(2,1)S(1)}, bf16[256,256]{1,0:T(8,128)(2,1)}, u32[]{:S(2)}) copy-start(bf16[256,256]{1,0:T(8,128)(2,1)} %param.14) | copy-start | bytes 393220
  7.2 326.7 %all-reduce.2.cloned.1.call-start = ((), (), s32[]{:S(2)}) async-start(), calls=%async_computation.1 | async-start | bytes 131072 | tf_op jit(solution)/shard_map/psum | solution.py:107
  9.9 2.3 copy-start.8
  11.2 1.4 copy-start.6
  12.1 1.3 copy-start.12
  12.1 1.3 copy-start.14
  13.5 2.0 copy-start.3
  15.4 3.0 copy-start.13
  25.2 8.3 %copy-start.2 = (bf16[4,1,256,1024]{3,2,0,1:T(8,128)(2,1)S(1)}, bf16[4,1,256,1024]{3,2,0,1:T(8,128)(2,1)}, u32[]{:S(2)}) copy-start(bf16[4,1,256,1024]{3,2,0,1:T(8,128)(2,1)} %convert_bitcast_fusion.1) | copy-start | bytes 6291460
  29.1 14.7 %collective-permute-start = (bf16[4,2,256,128]{3,2,0,1:T(8,128)(2,1)}, bf16[4,2,256,128]{3,2,0,1:T(8,128)(2,1)}, u32[]{:S(2)}, u32[]{:S(2)}) collective-permute-start(bf16[4,2,256,128]{3,2,0,1:T(8,128)(2,1)} %get-tuple-element.5), channel_id=1, source_target_pairs={{0,1},{1,0},{2,3},{3,2},{4,5},{5,4},{6,7},{7,6},{8,9},{9,8},{10,11... | collective-permute-start | bytes 1572872 | tf_op jit(solution)/shard_map/ppermute | solution.py:102
  29.1 19.4 %collective-permute-start.1 = (bf16[4,2,256,128]{3,2,0,1:T(8,128)(2,1)}, bf16[4,2,256,128]{3,2,0,1:T(8,128)(2,1)}, u32[]{:S(2)}, u32[]{:S(2)}) collective-permute-start(bf16[4,2,256,128]{3,2,0,1:T(8,128)(2,1)} %get-tuple-element.6), channel_id=1, source_target_pairs={{0,2},{1,3},{2,0},{3,1},{4,6},{5,7},{6,4},{7,5},{8,10},{9,11},{10,... | collective-permute-start | bytes 1572872 | tf_op jit(solution)/shard_map/ppermute | solution.py:102
  31.8 24.2 %collective-permute-start.2 = (bf16[4,2,256,128]{3,2,0,1:T(8,128)(2,1)}, bf16[4,2,256,128]{3,2,0,1:T(8,128)(2,1)}, u32[]{:S(2)}, u32[]{:S(2)}) collective-permute-start(bf16[4,2,256,128]{3,2,0,1:T(8,128)(2,1)} %get-tuple-element.7), channel_id=1, source_target_pairs={{0,3},{1,2},{2,1},{3,0},{4,7},{5,6},{6,5},{7,4},{8,11},{9,10},{10,... | collective-permute-start | bytes 1572872 | tf_op jit(solution)/shard_map/ppermute | solution.py:102
  31.9 26.6 %collective-permute-start.3 = (bf16[4,2,256,128]{3,2,0,1:T(8,128)(2,1)}, bf16[4,2,256,128]{3,2,0,1:T(8,128)(2,1)}, u32[]{:S(2)}, u32[]{:S(2)}) collective-permute-start(bf16[4,2,256,128]{3,2,0,1:T(8,128)(2,1)} %get-tuple-element.8), channel_id=1, source_target_pairs={{0,4},{1,5},{2,6},{3,7},{4,0},{5,1},{6,2},{7,3},{8,12},{9,13},{10,... | collective-permute-start | bytes 1572872 | tf_op jit(solution)/shard_map/ppermute | solution.py:102
  35.7 6.6 %copy-start.4 = (bf16[4,2,256,128]{3,2,0,1:T(8,128)(2,1)S(1)}, bf16[4,2,256,128]{3,2,0,1:T(8,128)(2,1)}, u32[]{:S(2)}) copy-start(bf16[4,2,256,128]{3,2,0,1:T(8,128)(2,1)} %get-tuple-element.4) | copy-start | bytes 1572868
  35.8 8.0 %copy-start.7 = (bf16[4,2,256,128]{3,2,0,1:T(8,128)(2,1)S(1)}, bf16[4,2,256,128]{3,2,0,1:T(8,128)(2,1)}, u32[]{:S(2)}) copy-start(bf16[4,2,256,128]{3,2,0,1:T(8,128)(2,1)} %get-tuple-element.9) | copy-start | bytes 1572868
  35.8 12.8 %copy-start.5 = (bf16[4,2,256,128]{3,2,0,1:T(8,128)(2,1)S(1)}, bf16[4,2,256,128]{3,2,0,1:T(8,128)(2,1)}, u32[]{:S(2)}) copy-start(bf16[4,2,256,128]{3,2,0,1:T(8,128)(2,1)} %get-tuple-element.3) | copy-start | bytes 1572868
  35.8 43.9 %collective-permute-start.4 = (bf16[4,2,256,128]{3,2,0,1:T(8,128)(2,1)}, bf16[4,2,256,128]{3,2,0,1:T(8,128)(2,1)S(1)}, u32[]{:S(2)}, u32[]{:S(2)}) collective-permute-start(bf16[4,2,256,128]{3,2,0,1:T(8,128)(2,1)} %get-tuple-element.10), channel_id=1, source_target_pairs={{0,5},{1,4},{2,7},{3,6},{4,1},{5,0},{6,3},{7,2},{8,13},{9,12},{10,... | collective-permute-start | bytes 1572872 | tf_op jit(solution)/shard_map/ppermute | solution.py:102
  43.7 37.3 %collective-permute-start.5 = (bf16[4,2,256,128]{3,2,0,1:T(8,128)(2,1)S(1)}, bf16[4,2,256,128]{3,2,0,1:T(8,128)(2,1)S(1)}, u32[]{:S(2)}, u32[]{:S(2)}) collective-permute-start(bf16[4,2,256,128]{3,2,0,1:T(8,128)(2,1)S(1)} %copy-done.7), channel_id=1, source_target_pairs={{0,6},{1,7},{2,4},{3,5},{4,2},{5,3},{6,0},{7,1},{8,14},{9,15},{10,... | collective-permute-start | bytes 1572872 | tf_op jit(solution)/shard_map/ppermute | solution.py:102
  48.6 33.9 %collective-permute-start.6 = (bf16[4,2,256,128]{3,2,0,1:T(8,128)(2,1)S(1)}, bf16[4,2,256,128]{3,2,0,1:T(8,128)(2,1)S(1)}, u32[]{:S(2)}, u32[]{:S(2)}) collective-permute-start(bf16[4,2,256,128]{3,2,0,1:T(8,128)(2,1)S(1)} %copy-done.5), channel_id=1, source_target_pairs={{0,7},{1,6},{2,5},{3,4},{4,3},{5,2},{6,1},{7,0},{8,15},{9,14},{10,... | collective-permute-start | bytes 1572872 | tf_op jit(solution)/shard_map/ppermute | solution.py:102
  194.3 3.2 copy-start.1
  197.5 17.1 %copy-start.11 = (f32[128]{0:T(128)S(1)}, f32[128]{0:T(128)}, u32[]{:S(2)}) copy-start(f32[128]{0:T(128)} %param.11) | copy-start | bytes 1540
  361.7 12.5 %copy-start.10 = (f32[128]{0:T(128)}, f32[128]{0:T(128)S(1)}, u32[]{:S(2)}) copy-start(f32[128]{0:T(128)S(1)} %fusion.21) | copy-start | bytes 1540
Sparse Core Ops, SparseCore 0:
  214.8 119.0 all-reduce.1
